TPU v7x, 128 devices: a whole 4x4x4 slice. The times are simulated.
128 devices in a mesh: gy: 16 (over x, y_lo, core), gx: 8 (over y_hi, z).
Axes of the slice: x: 4, y: 4 (y_hi: 2, y_lo: 2; y = y_hi * 2 + y_lo), z: 4, core: 2. Of those that a mesh axis runs over, the one named last changes fastest.
Arguments:
- tokens: bfloat16 [256, 512, 512], P('gy', 'gx'), may hold values from -6 to 6
- cotangent: bfloat16 [256, 512, 512], P('gy', 'gx'), may hold values from -6 to 6
- w_qkv: bfloat16 [512, 1536], replicated, may hold values from -0.25 to 0.25
- w_out: bfloat16 [512, 512], replicated, may hold values from -0.25 to 0.25
Outputs:
- grad_tokens: bfloat16 [256, 512, 512], P('gy', 'gx')
- grad_wqkv: float32 [512, 1536], P(('gy', 'gx'))
- grad_wout: float32 [512, 512], P(('gy', 'gx'))
All inputs are finite; a program needn't handle non-finite values.
Results may differ from a plain program's by a relative error of at most 0.0095.
Values may be sent and summed in bfloat16 or wider, within the bound.
A program may use at most 128 MiB of HBM per device.

v0:
```python
import functools

import jax
import jax.numpy as jnp
from jax import lax
from jax.experimental import pallas as pl
from jax.experimental.pallas import tpu as pltpu
from jax.sharding import PartitionSpec as P

MESH = pl.DeviceIdType.MESH
F32 = jnp.float32
BF16 = jnp.bfloat16

D = 512
HEADS = 16
HEAD = 32
EPS = 1e-05
CHIPS = 64
MEMBERS = 64
CHUNKS = 2
NW = 8
ROWS = NW * MEMBERS
STRIDE = 27
SCALE = HEAD ** (-0.5)
LOG2E = 1.4426950408889634
FACTOR = 131072.0 ** (-0.5)


def place():
    gy = lax.axis_index("gy")
    gx = lax.axis_index("gx")
    return gy // 4, (gx // 4) * 2 + (gy // 2) % 2, gx % 4, gy % 2


def device(x, y, z, core):
    return (x * 4 + (y % 2) * 2 + core, (y // 2) * 4 + z)


def shifted(here, k):
    x, y, z, core = here
    s = (k * STRIDE) % CHIPS
    return (x + s // 16) % 4, (y + (s // 4) % 4) % 4, (z + s % 4) % 4, core


def send_to_all(here, source, target, send_sem, recv_sem):
    me = here[0] * 16 + here[1] * 4 + here[2]

    def one(k, carry):
        x, y, z, core = shifted(here, k)
        chip = x * 16 + y * 4 + z
        pltpu.make_async_remote_copy(
            src_ref=source.at[chip],
            dst_ref=target.at[me],
            send_sem=send_sem,
            recv_sem=recv_sem,
            device_id=device(x, y, z, core),
            device_id_type=MESH,
        ).start()
        return carry

    lax.fori_loop(1, CHIPS, one, 0)
    target[me] = source[me]


def wait_all(buffer, sem):
    part = buffer.at[pl.ds(0, CHIPS - 1)]
    pltpu.make_async_copy(part, part, sem).wait()


def dot(a, b):
    return jnp.dot(a, b, preferred_element_type=F32)


def dot_t(a, b):
    return lax.dot_general(a, b, (((1,), (1,)), ((), ())), preferred_element_type=F32)


def dot_0(a, b):
    return lax.dot_general(a, b, (((0,), (0,)), ((), ())), preferred_element_type=F32)


def kernel(
    tok_hbm, cot_hbm, wqkv_hbm, wout_hbm,
    gt_ref, gw_ref, gwo_ref,
    tok, cot, wqkv, wout,
    sent, got, tok_f, cot_f, xhat, rstd, normed, cot_w, qkv, gatt, att, dqkv, gnorm, back_f,
    back, home, dw, dwo, part, other, summed, pieces,
    load_sem, in_send, in_recv, out_send, out_recv, x_send, x_recv, r_send, r_recv,
):
    here = place()
    core = here[3]
    me = here[0] * 16 + here[1] * 4 + here[2]

    loads = [
        pltpu.make_async_copy(tok_hbm, tok, load_sem.at[0]),
        pltpu.make_async_copy(cot_hbm, cot, load_sem.at[1]),
        pltpu.make_async_copy(wqkv_hbm, wqkv, load_sem.at[2]),
        pltpu.make_async_copy(wout_hbm, wout, load_sem.at[3]),
    ]
    for load in loads:
        load.start()

    barrier = pltpu.get_barrier_semaphore()

    def greet(k, carry):
        pl.semaphore_signal(barrier, inc=1, device_id=device(*shifted(here, k)), device_id_type=MESH)
        return carry

    lax.fori_loop(1, CHIPS, greet, 0)
    pl.semaphore_signal(
        barrier, inc=1, device_id=device(here[0], here[1], here[2], 1 - core), device_id_type=MESH
    )
    loads[0].wait()
    loads[1].wait()

    def pack(p, carry):
        cells = (p // 4, pl.ds(pl.multiple_of((p % 4) * 16, 16), 16))
        t = tok[cells].astype(F32)
        c = cot[cells].astype(F32)
        for i in range(CHUNKS):
            rows = slice(i * NW, (i + 1) * NW)
            sent[i, p] = jnp.concatenate([t[rows], c[rows]], axis=0).astype(BF16)
        return carry

    lax.fori_loop(0, CHIPS, pack, 0)
    pl.semaphore_wait(barrier, CHIPS)
    for i in range(CHUNKS):
        send_to_all(here, sent.at[i], got.at[i], in_send.at[i], in_recv.at[i])
    loads[2].wait()
    loads[3].wait()

    lane = lax.broadcasted_iota(jnp.int32, (MEMBERS, 128), 1) // HEAD

    for i in range(CHUNKS):
        wait_all(got.at[i], in_recv.at[i])

        def unpack(p, carry):
            block = got[i, p].astype(F32)
            rows = pl.ds(pl.multiple_of(p * NW, NW), NW)
            for t in range(4):
                lanes = slice(t * 128, (t + 1) * 128)
                tok_f[t, rows, :] = block[:NW, lanes]
                cot_f[t, rows, :] = block[NW:, lanes]
            return carry

        lax.fori_loop(0, CHIPS, unpack, 0)

        for j in range(NW):
            window = pl.ds(j * MEMBERS, MEMBERS)
            strided = pl.ds(j, MEMBERS, stride=NW)
            values = jnp.concatenate([tok_f[t, strided, :] for t in range(4)], axis=1)
            mean = jnp.mean(values, axis=-1, keepdims=True)
            centred = values - mean
            variance = jnp.mean(centred * centred, axis=-1, keepdims=True)
            inverse = lax.rsqrt(variance + EPS)
            standard = centred * inverse
            xhat[window, :] = standard
            rstd[window, :] = jnp.broadcast_to(inverse, (MEMBERS, 128))
            normed[window, :] = standard.astype(BF16)
            cot_w[window, :] = jnp.concatenate(
                [cot_f[t, strided, :] for t in range(4)], axis=1
            ).astype(BF16)

        for n in range(3):
            columns = slice(n * D, (n + 1) * D)
            qkv[:, columns] = dot(normed[...], wqkv[:, columns]).astype(BF16)
        gatt[...] = dot_t(cot_w[...], wout[...]).astype(BF16)

        def attend(w, carry):
            window = pl.ds(pl.multiple_of(w * MEMBERS, MEMBERS), MEMBERS)
            for g in range(4):
                lanes = [slice(n * D + g * 128, n * D + (g + 1) * 128) for n in range(3)]
                q, k, v = (qkv[window, lanes[n]] for n in range(3))
                go = gatt[window, lanes[0]]
                zero = jnp.zeros_like(q)
                qs = jnp.concatenate([jnp.where(lane == h, q, zero) for h in range(4)], axis=0)
                gs = jnp.concatenate([jnp.where(lane == h, go, zero) for h in range(4)], axis=0)
                s = dot_t(k, qs) * (SCALE * LOG2E)
                e = jnp.exp2(s - jnp.max(s, axis=0, keepdims=True))
                p = e * (1.0 / jnp.sum(e, axis=0, keepdims=True))
                gp = dot_t(v, gs)
                ds = p * (gp - jnp.sum(p * gp, axis=0, keepdims=True)) * SCALE
                ds = ds.astype(BF16)
                low = p.astype(BF16)
                dqkv[window, lanes[1]] = dot(ds, qs).astype(BF16)
                dqkv[window, lanes[2]] = dot(low, gs).astype(BF16)
                a4 = dot_0(low, v)
                q4 = dot_0(ds, k)

                def diagonal(blocks):
                    total = blocks[3 * MEMBERS :]
                    for h in range(3):
                        total = jnp.where(
                            lane == h, blocks[h * MEMBERS : (h + 1) * MEMBERS], total
                        )
                    return total.astype(BF16)

                att[window, lanes[0]] = diagonal(a4)
                dqkv[window, lanes[0]] = diagonal(q4)
            return carry

        lax.fori_loop(0, NW, attend, 0)

        for n in range(3):
            columns = slice(n * D, (n + 1) * D)
            term = dot_0(normed[...], dqkv[:, columns])
            dw[:, columns] = term if i == 0 else dw[:, columns] + term
        term = dot_0(att[...], cot_w[...])
        dwo[...] = term if i == 0 else dwo[...] + term

        if i == CHUNKS - 1:

            def regroup(t, carry):
                owner_x, y_lo, owner_core, y_hi, half = t // 16, (t // 8) % 2, (t // 4) % 2, (t // 2) % 2, t % 2
                rows = pl.ds(pl.multiple_of(t * 8, 8), 8)
                blocks = [dw[rows, n * D : (n + 1) * D] for n in range(3)] + [dwo[rows, :]]
                chip = owner_x * 16 + (y_hi * 2 + y_lo) * 4 + half * 2
                part[owner_core, chip] = jnp.concatenate([b[:4] for b in blocks], axis=0).astype(BF16)
                part[owner_core, chip + 1] = jnp.concatenate([b[4:] for b in blocks], axis=0).astype(BF16)
                return carry

            lax.fori_loop(0, D // 8, regroup, 0)
            cross = pltpu.make_async_remote_copy(
                src_ref=part.at[1 - core],
                dst_ref=other,
                send_sem=x_send,
                recv_sem=x_recv,
                device_id=device(here[0], here[1], here[2], 1 - core),
                device_id_type=MESH,
            )
            cross.start()

        gnorm[...] = dot_t(dqkv[...], wqkv[...])
        for j in range(NW):
            window = pl.ds(j * MEMBERS, MEMBERS)
            strided = pl.ds(j, MEMBERS, stride=NW)
            g = gnorm[window, :]
            standard = xhat[window, :]
            average = jnp.mean(g, axis=-1, keepdims=True)
            projected = jnp.mean(g * standard, axis=-1, keepdims=True)
            layer = rstd[window, 0:1] * (g - average - standard * projected)
            result = cot_w[window, :].astype(F32) + layer
            for t in range(4):
                back_f[t, strided, :] = result[:, t * 128 : (t + 1) * 128]

        def repack(p, carry):
            rows = pl.ds(pl.multiple_of(p * NW, NW), NW)
            left = jnp.concatenate([back_f[t, rows, :] for t in range(2)], axis=1)
            right = jnp.concatenate([back_f[t, rows, :] for t in range(2, 4)], axis=1)
            back[i, p] = jnp.concatenate([left, right], axis=0).astype(BF16)
            return carry

        lax.fori_loop(0, CHIPS, repack, 0)
        send_to_all(here, back.at[i], home.at[i], out_send.at[i], out_recv.at[i])

    cross.wait_recv()

    def pair(p, carry):
        summed[p] = (part[core, p].astype(F32) + other[p].astype(F32)).astype(BF16)
        return carry

    lax.fori_loop(0, CHIPS, pair, 0)
    send_to_all(here, summed, pieces, r_send, r_recv)

    for i in range(CHUNKS):
        wait_all(home.at[i], out_recv.at[i])

    def unfold(p, carry):
        halves = []
        for i in range(CHUNKS):
            block = home[i, p].astype(F32)
            halves.append(jnp.concatenate([block[:NW], block[NW:]], axis=1))
        cells = (p // 4, pl.ds(pl.multiple_of((p % 4) * 16, 16), 16))
        gt_ref[cells] = jnp.concatenate(halves, axis=0).astype(BF16)
        return carry

    lax.fori_loop(0, CHIPS, unfold, 0)

    wait_all(pieces, r_recv)
    total = lax.fori_loop(
        0, CHIPS, lambda p, acc: acc + pieces[p].astype(F32), jnp.zeros((16, D), F32)
    )
    total = total * FACTOR
    for n in range(3):
        gw_ref[:, n * D : (n + 1) * D] = total[n * 4 : (n + 1) * 4]
    gwo_ref[...] = total[12:]

    cross.wait_send()
    for i in range(CHUNKS):
        wait_all(sent.at[i], in_send.at[i])
        wait_all(back.at[i], out_send.at[i])
    wait_all(summed, r_send)


def body(tokens, cotangent, w_qkv, w_out):
    rows, columns, _ = tokens.shape
    vmem = pltpu.VMEM
    dma = pltpu.SemaphoreType.DMA
    return pl.pallas_call(
        kernel,
        out_shape=(
            jax.ShapeDtypeStruct((rows, columns, D), BF16),
            jax.ShapeDtypeStruct((4, 3 * D), F32),
            jax.ShapeDtypeStruct((4, D), F32),
        ),
        in_specs=[pl.BlockSpec(memory_space=pl.ANY)] * 4,
        out_specs=[pl.BlockSpec(memory_space=vmem)] * 3,
        scratch_shapes=[
            vmem((rows, columns, D), BF16),
            vmem((rows, columns, D), BF16),
            vmem((D, 3 * D), BF16),
            vmem((D, D), BF16),
            vmem((CHUNKS, CHIPS, 2 * NW, D), BF16),
            vmem((CHUNKS, CHIPS, 2 * NW, D), BF16),
            vmem((4, ROWS, 128), F32),
            vmem((4, ROWS, 128), F32),
            vmem((ROWS, D), F32),
            vmem((ROWS, 128), F32),
            vmem((ROWS, D), BF16),
            vmem((ROWS, D), BF16),
            vmem((ROWS, 3 * D), BF16),
            vmem((ROWS, D), BF16),
            vmem((ROWS, D), BF16),
            vmem((ROWS, 3 * D), BF16),
            vmem((ROWS, D), F32),
            vmem((4, ROWS, 128), F32),
            vmem((CHUNKS, CHIPS, 16, NW * D // 16), BF16),
            vmem((CHUNKS, CHIPS, 16, NW * D // 16), BF16),
            vmem((D, 3 * D), F32),
            vmem((D, D), F32),
            vmem((2, CHIPS, 16, D), BF16),
            vmem((CHIPS, 16, D), BF16),
            vmem((CHIPS, 16, D), BF16),
            vmem((CHIPS, 16, D), BF16),
            dma((4,)),
            dma((CHUNKS,)), dma((CHUNKS,)),
            dma((CHUNKS,)), dma((CHUNKS,)),
            dma(()), dma(()),
            dma(()), dma(()),
        ],
        compiler_params=pltpu.CompilerParams(
            collective_id=0, has_side_effects=True, vmem_limit_bytes=60 << 20
        ),
        name="grid_attention_backward",
    )(tokens, cotangent, w_qkv, w_out)


def solution(mesh):
    in_specs = (P("gy", "gx", None), P("gy", "gx", None), P(), P())
    out_specs = (P("gy", "gx", None), P(("gy", "gx"), None), P(("gy", "gx"), None))
    return jax.shard_map(body, mesh=mesh, in_specs=in_specs, out_specs=out_specs, check_vma=False)
```

profile of v0, /device:TPU:24, one launch (start us, length us, event | category | flops | bytes accessed | tf_op | source)
XLA Modules:
  0.0 93.3 jit_solution(8736884741786551214)
XLA Ops:
  0.6 89.1 %grid_attention_backward.1 = (bf16[16,64,512]{2,1,0:T(8,128)(2,1)}, f32[4,1536]{1,0:T(4,128)}, f32[4,512]{1,0:T(4,128)}) custom-call(bf16[16,64,512]{2,1,0:T(8,128)(2,1)} %tok_hbm.1, bf16[16,64,512]{2,1,0:T(8,128)(2,1)} %cot_hbm.1, bf16[512,1536]{1,0:T(8,128)(2,1)} %wqkv_hbm.1, bf16[512,512]{1,0:T(8,128)(2,1)} %wout_hbm.1), custom_call_target="tpu_custom_call" | custom-call | tf_op jit(solution)/shard_map/grid_attention_backward/pallas_call | solution.py:299
  89.8 0.0 copy-start
  89.8 0.0 copy-start.1
  89.8 2.3 %copy.10 = bf16[16,64,512]{2,1,0:T(8,128)(2,1)} copy(bf16[16,64,512]{2,1,0:T(8,128)(2,1)} %get-tuple-element.6) | data formatting | bytes 2097152
  92.1 0.0 copy-done
  92.1 0.6 copy.11
  92.7 0.0 copy-done.1
  92.7 0.6 copy.12
Async XLA Ops:
  89.8 2.3 %copy-start = (f32[4,1536]{1,0:T(4,128)S(1)}, f32[4,1536]{1,0:T(4,128)}, u32[]{:S(2)}) copy-start(f32[4,1536]{1,0:T(4,128)} %get-tuple-element.7) | copy-start | bytes 73732
  89.8 2.9 %copy-start.1 = (f32[4,512]{1,0:T(4,128)S(1)}, f32[4,512]{1,0:T(4,128)}, u32[]{:S(2)}) copy-start(f32[4,512]{1,0:T(4,128)} %get-tuple-element.8) | copy-start | bytes 24580
where the time goes:
time: 93.4 us; the launch traced here: 93.3 us
  Pallas kernels  89.1 us (95%)
  local copies, waits for them, and re-layouts  3.51 us (4%)
    pallas_call x1, Pallas kernels, body(): pl.pallas_call(kernel, out_shape=(jax.ShapeDtypeStruct((rows, columns, D)...  89.1 us
    unnamed x7, local copies, waits for them, and re-layouts  3.51 us

commit v1 on v0

v1 whole, which is shorter than its diff:
```python
import jax
import jax.numpy as jnp
from jax import lax
from jax.experimental import pallas as pl
from jax.experimental.pallas import tpu as pltpu
from jax.sharding import PartitionSpec as P

MESH = pl.DeviceIdType.MESH
F32 = jnp.float32
BF16 = jnp.bfloat16

D = 512
HEAD = 32
EPS = 1e-05
CHIPS = 64
MEMBERS = 64
WINDOWS = 16
CHUNKS = 2
NW = WINDOWS // CHUNKS
ROWS = NW * MEMBERS
KEEP = CHUNKS // 2
IN_LANES = 2 * NW * D // 16
OUT_LANES = NW * D // 16
TOGETHER = 2
SCALE = HEAD ** (-0.5)
LOG2E = 1.4426950408889634
FACTOR = 131072.0 ** (-0.5)


def place():
    gy = lax.axis_index("gy")
    gx = lax.axis_index("gx")
    return gy // 4, (gx // 4) * 2 + (gy // 2) % 2, gx % 4, gy % 2


def device(x, y, z, core):
    return (x * 4 + (y % 2) * 2 + core, (y // 2) * 4 + z)


def chip_of(x, y, z):
    return x * 16 + y * 4 + z


def moved(here, x, y, z):
    return (here[0] + x) % 4, (here[1] + y) % 4, (here[2] + z) % 4, here[3]


def for_line(here, act):
    def step(d, carry):
        act(moved(here, d, 0, 0))
        act(moved(here, 0, d, 0))
        act(moved(here, 0, 0, d))
        return carry

    lax.fori_loop(1, 4, step, 0)


def for_plane(here, act):
    def step(k, carry):
        a, b = k // 3 + 1, k % 3 + 1
        act(moved(here, a, b, 0))
        act(moved(here, 0, a, b))
        act(moved(here, b, 0, a))
        return carry

    lax.fori_loop(0, 9, step, 0)


def for_space(here, act):
    def step(k, carry):
        s = (k * 10) % 27
        act(moved(here, s // 9 + 1, (s // 3) % 3 + 1, s % 3 + 1))
        return carry

    lax.fori_loop(0, 27, step, 0)


def for_all(here, act):
    def step(k, carry):
        s = (k * 27) % CHIPS
        act(moved(here, s // 16, (s // 4) % 4, s % 4))
        return carry

    lax.fori_loop(1, CHIPS, step, 0)


def sender(here, source, target, send_sem, recv_sem):
    me = chip_of(*here[:3])

    def act(there):
        pltpu.make_async_remote_copy(
            src_ref=source.at[chip_of(*there[:3])],
            dst_ref=target.at[me],
            send_sem=send_sem,
            recv_sem=recv_sem,
            device_id=device(*there),
            device_id_type=MESH,
        ).start()

    return act


def wait_all(buffer, sem):
    part = buffer.at[pl.ds(0, CHIPS - 1)]
    pltpu.make_async_copy(part, part, sem).wait()


def dot(a, b):
    return jnp.dot(a, b, preferred_element_type=F32)


def dot_t(a, b):
    return lax.dot_general(a, b, (((1,), (1,)), ((), ())), preferred_element_type=F32)


def dot_0(a, b):
    return lax.dot_general(a, b, (((0,), (0,)), ((), ())), preferred_element_type=F32)


def fold(rows):
    n, width = rows.shape
    parts = 16 // n
    lanes = width // parts
    return jnp.concatenate([rows[:, i * lanes : (i + 1) * lanes] for i in range(parts)], axis=0)


def unfold(block, n):
    parts = 16 // n
    return jnp.concatenate([block[i * n : (i + 1) * n] for i in range(parts)], axis=1)


def attend(w, base, qkv, gatt, dqkv, att):
    lane = lax.broadcasted_iota(jnp.int32, (MEMBERS, 128), 1) // HEAD
    zero = jnp.zeros((MEMBERS, 128), BF16)

    def spread(a):
        return jnp.concatenate([jnp.where(lane == h, a, zero) for h in range(4)], axis=0)

    def diagonal(blocks):
        total = blocks[3 * MEMBERS :]
        for h in range(3):
            total = jnp.where(lane == h, blocks[h * MEMBERS : (h + 1) * MEMBERS], total)
        return total.astype(BF16)

    units = []
    for i in range(TOGETHER):
        start = (w * TOGETHER + i) * MEMBERS
        inside = pl.ds(pl.multiple_of(start, MEMBERS), MEMBERS)
        kept = pl.ds(pl.multiple_of(base + start, MEMBERS), MEMBERS)
        for g in range(4):
            units.append((inside, kept, [slice(n * D + g * 128, n * D + (g + 1) * 128) for n in range(3)]))
    qs = [spread(qkv[r, c[0]]) for r, _, c in units]
    gs = [spread(gatt[r, c[0]]) for r, _, c in units]
    s = [dot_t(qkv[r, c[1]], b) * (SCALE * LOG2E) for (r, _, c), b in zip(units, qs)]
    gp = [dot_t(qkv[r, c[2]], b) for (r, _, c), b in zip(units, gs)]
    e = [jnp.exp2(a - jnp.max(a, axis=0, keepdims=True)) for a in s]
    p = [a * (1.0 / jnp.sum(a, axis=0, keepdims=True)) for a in e]
    low = [a.astype(BF16) for a in p]
    ds = [
        (a * (b - jnp.sum(a * b, axis=0, keepdims=True)) * SCALE).astype(BF16)
        for a, b in zip(p, gp)
    ]
    for n, (r, kept, c) in enumerate(units):
        dqkv[kept, c[1]] = dot(ds[n], qs[n]).astype(BF16)
        dqkv[kept, c[2]] = dot(low[n], gs[n]).astype(BF16)
    for n, (r, kept, c) in enumerate(units):
        att[kept, c[0]] = diagonal(dot_0(low[n], qkv[r, c[2]]))
        dqkv[kept, c[0]] = diagonal(dot_0(ds[n], qkv[r, c[1]]))


def kernel(
    tok_hbm, cot_hbm, wqkv_hbm, wout_hbm,
    home, total_ref,
    tok, cot, wqkv, wout,
    sent, got, both_f, xhat, rstd, normed, cot_w, qkv, gatt, att, dqkv, gnorm, back_f,
    back, dw, dwo, part, other, summed, pieces,
    load_sem, line_sem, space_sem, own_sem,
    in_send, in_recv, out_send, out_recv, x_send, x_recv, r_send, r_recv,
):
    here = place()
    core = here[3]
    me = chip_of(*here[:3])
    partner = device(here[0], here[1], here[2], 1 - core)

    loads = [
        pltpu.make_async_copy(tok_hbm, tok, load_sem.at[0]),
        pltpu.make_async_copy(cot_hbm, cot, load_sem.at[1]),
        pltpu.make_async_copy(wqkv_hbm, wqkv, load_sem.at[2]),
        pltpu.make_async_copy(wout_hbm, wout, load_sem.at[3]),
    ]
    for load in loads:
        load.start()

    barrier = pltpu.get_barrier_semaphore()

    def signal(sem):
        return lambda there: pl.semaphore_signal(
            sem, inc=1, device_id=device(*there), device_id_type=MESH
        )

    for_line(here, signal(barrier))
    pl.semaphore_signal(barrier, inc=1, device_id=partner, device_id_type=MESH)
    loads[0].wait()
    loads[1].wait()

    def pack(p, carry):
        cells = (p // 4, pl.ds(pl.multiple_of((p % 4) * 16, 16), 16))
        t = tok[cells].astype(F32)
        c = cot[cells].astype(F32)
        for i in range(CHUNKS):
            rows = slice(i * NW, (i + 1) * NW)
            sent[i, p] = fold(jnp.concatenate([t[rows], c[rows]], axis=0)).astype(BF16)
        return carry

    lax.fori_loop(0, CHIPS, pack, 0, unroll=2)
    for i in range(CHUNKS):
        got[i, me] = sent[i, me]

    first = sender(here, sent.at[0], got.at[0], in_send.at[0], in_recv.at[0])
    pl.semaphore_wait(barrier, 10)
    for_line(here, signal(line_sem))
    for_line(here, first)
    pl.semaphore_wait(line_sem, 9)
    for d in range(1, 4):
        signal(space_sem)(moved(here, d, 0, 0))
    for_plane(here, first)
    pl.semaphore_wait(space_sem, 3)
    for_space(here, first)

    def send_in(i):
        for_all(here, sender(here, sent.at[i], got.at[i], in_send.at[i], in_recv.at[i]))

    send_in(1)
    loads[2].wait()
    loads[3].wait()

    for i in range(CHUNKS):
        wait_all(got.at[i], in_recv.at[i])
        if i + 2 < CHUNKS:
            send_in(i + 2)
        base = (i % KEEP) * ROWS
        kept = slice(base, base + ROWS)

        def unpack(p, carry):
            block = unfold(got[i, p].astype(F32), 2 * NW) if NW < 8 else got[i, p].astype(F32)
            rows = pl.ds(pl.multiple_of(p * 2 * NW, 8), 2 * NW)
            for t in range(4):
                both_f[t, rows, :] = block[:, t * 128 : (t + 1) * 128]
            return carry

        lax.fori_loop(0, CHIPS, unpack, 0, unroll=4)

        for j in range(NW):
            window = slice(j * MEMBERS, (j + 1) * MEMBERS)
            members = pl.ds(j, MEMBERS, stride=2 * NW)
            values = jnp.concatenate([both_f[t, members, :] for t in range(4)], axis=1)
            mean = jnp.mean(values, axis=-1, keepdims=True)
            centred = values - mean
            variance = jnp.mean(centred * centred, axis=-1, keepdims=True)
            inverse = lax.rsqrt(variance + EPS)
            standard = centred * inverse
            xhat[window, :] = standard
            rstd[window, :] = jnp.broadcast_to(inverse, (MEMBERS, 128))
            low = slice(base + j * MEMBERS, base + (j + 1) * MEMBERS)
            normed[low, :] = standard.astype(BF16)
            members = pl.ds(NW + j, MEMBERS, stride=2 * NW)
            cot_w[low, :] = jnp.concatenate(
                [both_f[t, members, :] for t in range(4)], axis=1
            ).astype(BF16)

        for n in range(3):
            columns = slice(n * D, (n + 1) * D)
            qkv[:, columns] = dot(normed[kept, :], wqkv[:, columns]).astype(BF16)
        gatt[...] = dot_t(cot_w[kept, :], wout[...]).astype(BF16)

        def attention(w, carry):
            attend(w, base, qkv, gatt, dqkv, att)
            return carry

        lax.fori_loop(0, NW // TOGETHER, attention, 0)

        if i % KEEP == KEEP - 1:
            for n in range(3):
                columns = slice(n * D, (n + 1) * D)
                term = dot_0(normed[...], dqkv[:, columns])
                dw[:, columns] = term if i < KEEP else dw[:, columns] + term
            term = dot_0(att[...], cot_w[...])
            dwo[...] = term if i < KEEP else dwo[...] + term

        if i == CHUNKS - 1:

            def regroup(owner_core):
                def step(t, carry):
                    x, y_lo, y_hi, half = t // 8, (t // 4) % 2, (t // 2) % 2, t % 2
                    tile = x * 16 + y_lo * 8 + owner_core * 4 + y_hi * 2 + half
                    rows = pl.ds(pl.multiple_of(tile * 8, 8), 8)
                    blocks = [dw[rows, n * D : (n + 1) * D] for n in range(3)] + [dwo[rows, :]]
                    chip = chip_of(x, y_hi * 2 + y_lo, half * 2)
                    for k in range(2):
                        piece = [b[k * 4 : (k + 1) * 4] for b in blocks]
                        part[owner_core, chip + k] = jnp.concatenate(piece, axis=0).astype(BF16)
                    return carry

                lax.fori_loop(0, CHIPS // 2, step, 0, unroll=2)

            regroup(1 - core)
            cross = pltpu.make_async_remote_copy(
                src_ref=part.at[1 - core],
                dst_ref=other,
                send_sem=x_send,
                recv_sem=x_recv,
                device_id=partner,
                device_id_type=MESH,
            )
            cross.start()
            regroup(core)

        gnorm[...] = dot_t(dqkv[kept, :], wqkv[...])
        for j in range(NW):
            window = slice(j * MEMBERS, (j + 1) * MEMBERS)
            members = pl.ds(j, MEMBERS, stride=NW)
            g = gnorm[window, :]
            standard = xhat[window, :]
            average = jnp.mean(g, axis=-1, keepdims=True)
            projected = jnp.mean(g * standard, axis=-1, keepdims=True)
            layer = rstd[window, 0:1] * (g - average - standard * projected)
            result = cot_w[base + j * MEMBERS : base + (j + 1) * MEMBERS, :].astype(F32) + layer
            for t in range(4):
                back_f[t, members, :] = result[:, t * 128 : (t + 1) * 128]

        def repack(b, carry):
            rows = pl.ds(pl.multiple_of(b * 8, 8), 8)
            block = jnp.concatenate([back_f[t, rows, :] for t in range(4)], axis=1)
            for k in range(8 // NW):
                back[i, b * (8 // NW) + k] = fold(block[k * NW : (k + 1) * NW]).astype(BF16)
            return carry

        lax.fori_loop(0, ROWS // 8, repack, 0, unroll=2)
        for_all(here, sender(here, back.at[i], home.at[i], out_send.at[i], out_recv.at[i]))
        pltpu.make_async_copy(back.at[i, me], home.at[i, me], own_sem.at[i]).start()

    cross.wait_recv()

    def pair(b, carry):
        for k in range(4):
            p = b * 4 + k
            summed[p] = (part[core, p].astype(F32) + other[p].astype(F32)).astype(BF16)
        return carry

    lax.fori_loop(0, CHIPS // 4, pair, 0)
    for_all(here, sender(here, summed, pieces, r_send, r_recv))
    pieces[me] = summed[me]

    for i in range(CHUNKS):
        wait_all(home.at[i], out_recv.at[i])
        pltpu.make_async_copy(back.at[i, me], home.at[i, me], own_sem.at[i]).wait()
    wait_all(pieces, r_recv)

    def add(b, acc):
        for k in range(4):
            acc = acc + pieces[b * 4 + k].astype(F32)
        return acc

    total_ref[...] = lax.fori_loop(0, CHIPS // 4, add, jnp.zeros((16, D), F32))

    cross.wait_send()
    for i in range(CHUNKS):
        wait_all(sent.at[i], in_send.at[i])
        wait_all(back.at[i], out_send.at[i])
    wait_all(summed, r_send)


def finish(home, total, gt, gw, gwo):
    def cells(b, carry):
        p = pl.ds(b, 1)
        blocks = [home[i, p][0].astype(F32) for i in range(CHUNKS)]
        value = jnp.concatenate([unfold(block, NW) for block in blocks], axis=0)
        gt[b // 4, pl.ds(pl.multiple_of((b % 4) * 16, 16), 16)] = value.astype(BF16)
        return carry

    lax.fori_loop(0, 16, cells, 0, unroll=4)

    @pl.when(pl.program_id(0) == 0)
    def _():
        scaled = total[...] * FACTOR
        for n in range(3):
            gw[:, n * D : (n + 1) * D] = scaled[n * 4 : (n + 1) * 4]
        gwo[...] = scaled[12:]


def body(tokens, cotangent, w_qkv, w_out):
    rows, columns, _ = tokens.shape
    vmem = pltpu.VMEM
    dma = pltpu.SemaphoreType.DMA
    regular = pltpu.SemaphoreType.REGULAR
    home, total = pl.pallas_call(
        kernel,
        out_shape=(
            jax.ShapeDtypeStruct((CHUNKS, CHIPS, 16, OUT_LANES), BF16),
            jax.ShapeDtypeStruct((16, D), F32),
        ),
        in_specs=[pl.BlockSpec(memory_space=pl.ANY)] * 4,
        out_specs=[pl.BlockSpec(memory_space=pl.ANY), pl.BlockSpec(memory_space=vmem)],
        scratch_shapes=[
            vmem((rows, columns, D), BF16),
            vmem((rows, columns, D), BF16),
            vmem((D, 3 * D), BF16),
            vmem((D, D), BF16),
            vmem((CHUNKS, CHIPS, 16, IN_LANES), BF16),
            vmem((CHUNKS, CHIPS, 16, IN_LANES), BF16),
            vmem((4, 2 * ROWS, 128), F32),
            vmem((ROWS, D), F32),
            vmem((ROWS, 128), F32),
            vmem((KEEP * ROWS, D), BF16),
            vmem((KEEP * ROWS, D), BF16),
            vmem((ROWS, 3 * D), BF16),
            vmem((ROWS, D), BF16),
            vmem((KEEP * ROWS, D), BF16),
            vmem((KEEP * ROWS, 3 * D), BF16),
            vmem((ROWS, D), F32),
            vmem((4, ROWS, 128), F32),
            vmem((CHUNKS, CHIPS, 16, OUT_LANES), BF16),
            vmem((D, 3 * D), F32),
            vmem((D, D), F32),
            vmem((2, CHIPS, 16, D), BF16),
            vmem((CHIPS, 16, D), BF16),
            vmem((CHIPS, 16, D), BF16),
            vmem((CHIPS, 16, D), BF16),
            dma((4,)), regular, regular, dma((CHUNKS,)),
            dma((CHUNKS,)), dma((CHUNKS,)),
            dma((CHUNKS,)), dma((CHUNKS,)),
            dma(()), dma(()),
            dma(()), dma(()),
        ],
        compiler_params=pltpu.CompilerParams(
            collective_id=0, has_side_effects=True, vmem_limit_bytes=60 << 20
        ),
        name="grid_attention_backward",
    )(tokens, cotangent, w_qkv, w_out)
    steps = 4
    return pl.pallas_call(
        finish,
        grid=(steps,),
        out_shape=(
            jax.ShapeDtypeStruct((rows, columns, D), BF16),
            jax.ShapeDtypeStruct((4, 3 * D), F32),
            jax.ShapeDtypeStruct((4, D), F32),
        ),
        in_specs=[
            pl.BlockSpec((CHUNKS, CHIPS // steps, 16, OUT_LANES), lambda s: (0, s, 0, 0)),
            pl.BlockSpec((16, D), lambda s: (0, 0)),
        ],
        out_specs=[
            pl.BlockSpec((rows // steps, columns, D), lambda s: (s, 0, 0)),
            pl.BlockSpec((4, 3 * D), lambda s: (0, 0)),
            pl.BlockSpec((4, D), lambda s: (0, 0)),
        ],
        compiler_params=pltpu.CompilerParams(vmem_limit_bytes=60 << 20),
        name="cells_from_blocks",
    )(home, total)


def solution(mesh):
    in_specs = (P("gy", "gx", None), P("gy", "gx", None), P(), P())
    out_specs = (P("gy", "gx", None), P(("gy", "gx"), None), P(("gy", "gx"), None))
    return jax.shard_map(body, mesh=mesh, in_specs=in_specs, out_specs=out_specs, check_vma=False)
```

time: 93.4 us -> 72.3 us (0.77)
  the two profiles are of different devices: /device:TPU:24 before, /device:TPU:0 now
where the time goes in v1:
time: 72.3 us; the launch traced here: 71.7 us
  Pallas kernels  71 us (98%)
    pallas_call x1, Pallas kernels, body(): pl.pallas_call(kernel, out_shape=(jax.ShapeDtypeStruct((CHUNKS, CHIPS, 16...  67.5 us
    pallas_call x1, Pallas kernels, body(): pl.pallas_call(finish, grid=(steps,), out_shape=(jax.ShapeDtypeStruct((ro...  3.56 us

profile of v1, /device:TPU:0, one launch (start us, length us, event | category | flops | bytes accessed | tf_op | source)
XLA Modules:
  0.0 71.7 jit_solution(9486634959344273293)
XLA Ops:
  0.6 67.5 %grid_attention_backward.1 = (bf16[2,64,16,256]{3,2,1,0:T(8,128)(2,1)}, f32[16,512]{1,0:T(8,128)}) custom-call(bf16[16,64,512]{2,1,0:T(8,128)(2,1)} %tok_hbm.1, bf16[16,64,512]{2,1,0:T(8,128)(2,1)} %cot_hbm.1, bf16[512,1536]{1,0:T(8,128)(2,1)} %wqkv_hbm.1, bf16[512,512]{1,0:T(8,128)(2,1)} %wout_hbm.1), custom_call_target="tpu_custom_call" | custom-call | tf_op jit(solution)/shard_map/grid_attention_backward/pallas_call | solution.py:396
  68.1 3.6 %cells_from_blocks.1 = (bf16[16,64,512]{2,1,0:T(8,128)(2,1)}, f32[4,1536]{1,0:T(4,128)}, f32[4,512]{1,0:T(4,128)}) custom-call(bf16[2,64,16,256]{3,2,1,0:T(8,128)(2,1)} %get-tuple-element.5.home, f32[16,512]{1,0:T(8,128)} %get-tuple-element.6.total), custom_call_target="tpu_custom_call" | custom-call | tf_op jit(solution)/shard_map/cells_from_blocks/pallas_call | solution.py:441

commit v2 on v1

--- a/solution.py
+++ b/solution.py
@@ -21,7 +21,7 @@
 KEEP = CHUNKS // 2
 IN_LANES = 2 * NW * D // 16
 OUT_LANES = NW * D // 16
-TOGETHER = 2
+TOGETHER = 4
 SCALE = HEAD ** (-0.5)
 LOG2E = 1.4426950408889634
 FACTOR = 131072.0 ** (-0.5)
@@ -173,9 +173,10 @@
     home, total_ref,
     tok, cot, wqkv, wout,
     sent, got, both_f, xhat, rstd, normed, cot_w, qkv, gatt, att, dqkv, gnorm, back_f,
-    back, dw, dwo, part, other, summed, pieces,
+    back, dw, dwo, given, taken,
+    left, right, left_in, right_in, left_sum, right_sum, left_all, right_all,
     load_sem, line_sem, space_sem, own_sem,
-    in_send, in_recv, out_send, out_recv, x_send, x_recv, r_send, r_recv,
+    in_send, in_recv, out_send, out_recv, x_send, x_recv, a_send, a_recv, b_send, b_recv,
 ):
     here = place()
     core = here[3]
@@ -289,31 +290,22 @@
 
         if i == CHUNKS - 1:
 
-            def regroup(owner_core):
-                def step(t, carry):
-                    x, y_lo, y_hi, half = t // 8, (t // 4) % 2, (t // 2) % 2, t % 2
-                    tile = x * 16 + y_lo * 8 + owner_core * 4 + y_hi * 2 + half
-                    rows = pl.ds(pl.multiple_of(tile * 8, 8), 8)
-                    blocks = [dw[rows, n * D : (n + 1) * D] for n in range(3)] + [dwo[rows, :]]
-                    chip = chip_of(x, y_hi * 2 + y_lo, half * 2)
-                    for k in range(2):
-                        piece = [b[k * 4 : (k + 1) * 4] for b in blocks]
-                        part[owner_core, chip + k] = jnp.concatenate(piece, axis=0).astype(BF16)
-                    return carry
-
-                lax.fori_loop(0, CHIPS // 2, step, 0, unroll=2)
-
-            regroup(1 - core)
+            def lower(b, carry):
+                rows = pl.ds(pl.multiple_of(b * 64 + (1 - core) * 32, 32), 32)
+                given[b, :, : 3 * D] = dw[rows, :].astype(BF16)
+                given[b, :, 3 * D :] = dwo[rows, :].astype(BF16)
+                return carry
+
+            lax.fori_loop(0, 8, lower, 0)
             cross = pltpu.make_async_remote_copy(
-                src_ref=part.at[1 - core],
-                dst_ref=other,
+                src_ref=given,
+                dst_ref=taken,
                 send_sem=x_send,
                 recv_sem=x_recv,
                 device_id=partner,
                 device_id_type=MESH,
             )
             cross.start()
-            regroup(core)
 
         gnorm[...] = dot_t(dqkv[kept, :], wqkv[...])
         for j in range(NW):
@@ -341,33 +333,102 @@
 
     cross.wait_recv()
 
-    def pair(b, carry):
-        for k in range(4):
-            p = b * 4 + k
-            summed[p] = (part[core, p].astype(F32) + other[p].astype(F32)).astype(BF16)
-        return carry
-
-    lax.fori_loop(0, CHIPS // 4, pair, 0)
-    for_all(here, sender(here, summed, pieces, r_send, r_recv))
-    pieces[me] = summed[me]
+    def halves(owner_x):
+        def step(b, carry):
+            y_lo, y_hi = b // 2, b % 2
+            block = owner_x * 2 + y_lo
+            rows = pl.ds(pl.multiple_of(block * 64 + core * 32 + y_hi * 16, 16), 16)
+            theirs = taken[block, pl.ds(pl.multiple_of(y_hi * 16, 16), 16), :].astype(F32)
+            mine = jnp.concatenate([dw[rows, :], dwo[rows, :]], axis=1) + theirs
+            y = y_hi * 2 + y_lo
+            for z in range(4):
+                piece = jnp.concatenate(
+                    [mine[z * 4 : (z + 1) * 4, n * D : (n + 1) * D] for n in range(4)], axis=0
+                ).astype(BF16)
+                left[owner_x * 16 + y * 4 + z] = piece[:, : D // 2]
+                right[y * 16 + owner_x * 4 + z] = piece[:, D // 2 :]
+            return carry
+
+        lax.fori_loop(0, 4, step, 0)
+
+    def quarter(source, target, k, sem, there):
+        return pltpu.make_async_remote_copy(
+            src_ref=source.at[pl.ds(pl.multiple_of(k * 16, 16), 16)],
+            dst_ref=target,
+            send_sem=a_send.at[sem],
+            recv_sem=a_recv.at[sem],
+            device_id=device(*there),
+            device_id_type=MESH,
+        )
+
+    for d in range(1, 4):
+        there = moved(here, d, 0, 0)
+        halves(there[0])
+        quarter(left, left_in.at[here[0]], there[0], 0, there).start()
+    halves(here[0])
+    for d in range(1, 4):
+        there = moved(here, 0, d, 0)
+        quarter(right, right_in.at[here[1]], there[1], 1, there).start()
+
+    def plane_sum(held, arrived, mine, target):
+        def step(q, carry):
+            value = held[mine * 16 + q].astype(F32)
+            for d in range(1, 4):
+                value = value + arrived[(mine + d) % 4, q].astype(F32)
+            target[q] = value.astype(BF16)
+            return carry
+
+        lax.fori_loop(0, 16, step, 0, unroll=2)
+
+    def scatter(source, target, sem, own, place_of):
+        def step(k, carry):
+            q = (own + k * 7) % 16
+            pltpu.make_async_remote_copy(
+                src_ref=source.at[q],
+                dst_ref=target.at[own],
+                send_sem=b_send.at[sem],
+                recv_sem=b_recv.at[sem],
+                device_id=device(*place_of(q // 4, q % 4)),
+                device_id_type=MESH,
+            ).start()
+            return carry
+
+        lax.fori_loop(1, 16, step, 0)
+        target[own] = source[own]
+
+    def three(buffer, sem):
+        part = buffer.at[pl.ds(0, 3)]
+        pltpu.make_async_copy(part, part, sem).wait()
+
+    def fifteen(buffer, sem):
+        part = buffer.at[pl.ds(0, 15)]
+        pltpu.make_async_copy(part, part, sem).wait()
+
+    three(left_in, a_recv.at[0])
+    plane_sum(left, left_in, here[0], left_sum)
+    scatter(left_sum, left_all, 0, here[1] * 4 + here[2], lambda a, b: (here[0], a, b, core))
+    three(right_in, a_recv.at[1])
+    plane_sum(right, right_in, here[1], right_sum)
+    scatter(right_sum, right_all, 1, here[0] * 4 + here[2], lambda a, b: (a, here[1], b, core))
 
     for i in range(CHUNKS):
         wait_all(home.at[i], out_recv.at[i])
         pltpu.make_async_copy(back.at[i, me], home.at[i, me], own_sem.at[i]).wait()
-    wait_all(pieces, r_recv)
-
-    def add(b, acc):
-        for k in range(4):
-            acc = acc + pieces[b * 4 + k].astype(F32)
-        return acc
-
-    total_ref[...] = lax.fori_loop(0, CHIPS // 4, add, jnp.zeros((16, D), F32))
+    for n, buffer in enumerate((left_all, right_all)):
+        fifteen(buffer, b_recv.at[n])
+        value = buffer[0].astype(F32)
+        for q in range(1, 16):
+            value = value + buffer[q].astype(F32)
+        total_ref[:, n * (D // 2) : (n + 1) * (D // 2)] = value
 
     cross.wait_send()
     for i in range(CHUNKS):
         wait_all(sent.at[i], in_send.at[i])
         wait_all(back.at[i], out_send.at[i])
-    wait_all(summed, r_send)
+    three(left_in, a_send.at[0])
+    three(right_in, a_send.at[1])
+    fifteen(left_all, b_send.at[0])
+    fifteen(right_all, b_send.at[1])
 
 
 def finish(home, total, gt, gw, gwo):
@@ -378,7 +439,7 @@
         gt[b // 4, pl.ds(pl.multiple_of((b % 4) * 16, 16), 16)] = value.astype(BF16)
         return carry
 
-    lax.fori_loop(0, 16, cells, 0, unroll=4)
+    lax.fori_loop(0, home.shape[1], cells, 0, unroll=4)
 
     @pl.when(pl.program_id(0) == 0)
     def _():
@@ -422,22 +483,29 @@
             vmem((CHUNKS, CHIPS, 16, OUT_LANES), BF16),
             vmem((D, 3 * D), F32),
             vmem((D, D), F32),
-            vmem((2, CHIPS, 16, D), BF16),
-            vmem((CHIPS, 16, D), BF16),
-            vmem((CHIPS, 16, D), BF16),
-            vmem((CHIPS, 16, D), BF16),
+            vmem((8, 32, 4 * D), BF16),
+            vmem((8, 32, 4 * D), BF16),
+            vmem((CHIPS, 16, D // 2), BF16),
+            vmem((CHIPS, 16, D // 2), BF16),
+            vmem((4, 16, 16, D // 2), BF16),
+            vmem((4, 16, 16, D // 2), BF16),
+            vmem((16, 16, D // 2), BF16),
+            vmem((16, 16, D // 2), BF16),
+            vmem((16, 16, D // 2), BF16),
+            vmem((16, 16, D // 2), BF16),
             dma((4,)), regular, regular, dma((CHUNKS,)),
             dma((CHUNKS,)), dma((CHUNKS,)),
             dma((CHUNKS,)), dma((CHUNKS,)),
             dma(()), dma(()),
-            dma(()), dma(()),
+            dma((2,)), dma((2,)),
+            dma((2,)), dma((2,)),
         ],
         compiler_params=pltpu.CompilerParams(
             collective_id=0, has_side_effects=True, vmem_limit_bytes=60 << 20
         ),
         name="grid_attention_backward",
     )(tokens, cotangent, w_qkv, w_out)
-    steps = 4
+    steps = 2
     return pl.pallas_call(
         finish,
         grid=(steps,),

time: 72.3 us -> 67.7 us (0.936)
  Pallas kernels: 71 us -> 66.9 us
    pallas_call x1, Pallas kernels: 67.5 us -> 64.5 us  [body(): pl.pallas_call(kernel, out_shape=(jax.ShapeDtypeStruct((CHUNKS, CHIPS, 16...]
    pallas_call x1, Pallas kernels: 3.56 us -> 2.39 us  [body(): pl.pallas_call(finish, grid=(steps,), out_shape=(jax.ShapeDtypeStruct((ro...]
where the time goes in v2:
time: 67.7 us; the launch traced here: 67.6 us
  Pallas kernels  66.9 us (99%)
    pallas_call x1, Pallas kernels, body(): pl.pallas_call(kernel, out_shape=(jax.ShapeDtypeStruct((CHUNKS, CHIPS, 16...  64.5 us
    pallas_call x1, Pallas kernels, body(): pl.pallas_call(finish, grid=(steps,), out_shape=(jax.ShapeDtypeStruct((ro...  2.39 us

profile of v2, /device:TPU:0, one launch (start us, length us, event | category | flops | bytes accessed | tf_op | source)
XLA Modules:
  0.0 67.6 jit_solution(4399780299165494466)
XLA Ops:
  0.6 64.5 %grid_attention_backward.1 = (bf16[2,64,16,256]{3,2,1,0:T(8,128)(2,1)}, f32[16,512]{1,0:T(8,128)}) custom-call(bf16[16,64,512]{2,1,0:T(8,128)(2,1)} %tok_hbm.1, bf16[16,64,512]{2,1,0:T(8,128)(2,1)} %cot_hbm.1, bf16[512,1536]{1,0:T(8,128)(2,1)} %wqkv_hbm.1, bf16[512,512]{1,0:T(8,128)(2,1)} %wout_hbm.1), custom_call_target="tpu_custom_call" | custom-call | tf_op jit(solution)/shard_map/grid_attention_backward/pallas_call | solution.py:457
  65.2 2.4 %cells_from_blocks.1 = (bf16[16,64,512]{2,1,0:T(8,128)(2,1)}, f32[4,1536]{1,0:T(4,128)}, f32[4,512]{1,0:T(4,128)}) custom-call(bf16[2,64,16,256]{3,2,1,0:T(8,128)(2,1)} %get-tuple-element.5.home, f32[16,512]{1,0:T(8,128)} %get-tuple-element.6.total), custom_call_target="tpu_custom_call" | custom-call | tf_op jit(solution)/shard_map/cells_from_blocks/pallas_call | solution.py:509

commit v3 on v1

--- a/solution.py
+++ b/solution.py
@@ -1,3 +1,5 @@
+import random
+
 import jax
 import jax.numpy as jnp
 from jax import lax
@@ -15,13 +17,13 @@
 CHIPS = 64
 MEMBERS = 64
 WINDOWS = 16
-CHUNKS = 2
+CHUNKS = 4
 NW = WINDOWS // CHUNKS
 ROWS = NW * MEMBERS
 KEEP = CHUNKS // 2
 IN_LANES = 2 * NW * D // 16
 OUT_LANES = NW * D // 16
-TOGETHER = 2
+TOGETHER = 4
 SCALE = HEAD ** (-0.5)
 LOG2E = 1.4426950408889634
 FACTOR = 131072.0 ** (-0.5)
@@ -45,59 +47,46 @@
     return (here[0] + x) % 4, (here[1] + y) % 4, (here[2] + z) % 4, here[3]
 
 
-def for_line(here, act):
-    def step(d, carry):
-        act(moved(here, d, 0, 0))
-        act(moved(here, 0, d, 0))
-        act(moved(here, 0, 0, d))
-        return carry
-
-    lax.fori_loop(1, 4, step, 0)
-
-
-def for_plane(here, act):
-    def step(k, carry):
-        a, b = k // 3 + 1, k % 3 + 1
-        act(moved(here, a, b, 0))
-        act(moved(here, 0, a, b))
-        act(moved(here, b, 0, a))
-        return carry
-
-    lax.fori_loop(0, 9, step, 0)
-
-
-def for_space(here, act):
-    def step(k, carry):
-        s = (k * 10) % 27
-        act(moved(here, s // 9 + 1, (s // 3) % 3 + 1, s % 3 + 1))
-        return carry
-
-    lax.fori_loop(0, 27, step, 0)
-
-
-def for_all(here, act):
-    def step(k, carry):
-        s = (k * 27) % CHIPS
-        act(moved(here, s // 16, (s // 4) % 4, s % 4))
-        return carry
-
-    lax.fori_loop(1, CHIPS, step, 0)
-
-
-def sender(here, source, target, send_sem, recv_sem):
-    me = chip_of(*here[:3])
-
-    def act(there):
+SHIFTS = [(k // 16, (k // 4) % 4, k % 4) for k in range(1, CHIPS)]
+random.Random(1).shuffle(SHIFTS)
+PLANE_SHIFTS = [(s[1], s[2]) for s in SHIFTS if s[0] == 0]
+LINE, PLANE, SPACE = ([s for s in SHIFTS if 3 - s.count(0) == n] for n in (1, 2, 3))
+
+
+class Places:
+    def __init__(self, here):
+        along = [[(here[a] + d) % 4 for d in range(4)] for a in range(3)]
+        self.core = here[3]
+        self.along = along
+        self.x_chip = [x * 16 for x in along[0]]
+        self.x_gy = [x * 4 + self.core for x in along[0]]
+        self.y_chip = [y * 4 for y in along[1]]
+        self.y_gy = [(y % 2) * 2 for y in along[1]]
+        self.y_gx = [(y // 2) * 4 for y in along[1]]
+        self.z = along[2]
+
+    def chip(self, s):
+        return self.x_chip[s[0]] + (self.y_chip[s[1]] + self.z[s[2]])
+
+    def at(self, s):
+        return [self.along[a][s[a]] for a in range(3)]
+
+    def device(self, s):
+        return self.x_gy[s[0]] + self.y_gy[s[1]], self.y_gx[s[1]] + self.z[s[2]]
+
+
+def send(places, shifts, source, target, send_sem, recv_sem):
+    me = places.chip((0, 0, 0))
+    landing = target.at[me]
+    for s in shifts:
         pltpu.make_async_remote_copy(
-            src_ref=source.at[chip_of(*there[:3])],
-            dst_ref=target.at[me],
+            src_ref=source.at[places.chip(s)],
+            dst_ref=landing,
             send_sem=send_sem,
             recv_sem=recv_sem,
-            device_id=device(*there),
+            device_id=places.device(s),
             device_id_type=MESH,
         ).start()
-
-    return act
 
 
 def wait_all(buffer, sem):
@@ -173,12 +162,14 @@
     home, total_ref,
     tok, cot, wqkv, wout,
     sent, got, both_f, xhat, rstd, normed, cot_w, qkv, gatt, att, dqkv, gnorm, back_f,
-    back, dw, dwo, part, other, summed, pieces,
+    back, dw, given, taken,
+    parts, line_in, line_sum, plane_in, straight,
     load_sem, line_sem, space_sem, own_sem,
-    in_send, in_recv, out_send, out_recv, x_send, x_recv, r_send, r_recv,
+    in_send, in_recv, out_send, out_recv, x_send, x_recv, a_send, a_recv, b_send, b_recv, r_send, r_recv,
 ):
     here = place()
     core = here[3]
+    places = Places(here)
     me = chip_of(*here[:3])
     partner = device(here[0], here[1], here[2], 1 - core)
 
@@ -193,12 +184,11 @@
 
     barrier = pltpu.get_barrier_semaphore()
 
-    def signal(sem):
-        return lambda there: pl.semaphore_signal(
-            sem, inc=1, device_id=device(*there), device_id_type=MESH
-        )
-
-    for_line(here, signal(barrier))
+    def signal(sem, shifts):
+        for s in shifts:
+            pl.semaphore_signal(sem, inc=1, device_id=places.device(s), device_id_type=MESH)
+
+    signal(barrier, LINE)
     pl.semaphore_signal(barrier, inc=1, device_id=partner, device_id_type=MESH)
     loads[0].wait()
     loads[1].wait()
@@ -216,28 +206,48 @@
     for i in range(CHUNKS):
         got[i, me] = sent[i, me]
 
-    first = sender(here, sent.at[0], got.at[0], in_send.at[0], in_recv.at[0])
+    def send_in(i, shifts):
+        send(places, shifts, sent.at[i], got.at[i], in_send.at[i], in_recv.at[i])
+
     pl.semaphore_wait(barrier, 10)
-    for_line(here, signal(line_sem))
-    for_line(here, first)
+    signal(line_sem, LINE)
+    for i in range(2):
+        send_in(i, LINE)
     pl.semaphore_wait(line_sem, 9)
-    for d in range(1, 4):
-        signal(space_sem)(moved(here, d, 0, 0))
-    for_plane(here, first)
+    signal(space_sem, [(d, 0, 0) for d in range(1, 4)])
+    send_in(0, PLANE)
     pl.semaphore_wait(space_sem, 3)
-    for_space(here, first)
-
-    def send_in(i):
-        for_all(here, sender(here, sent.at[i], got.at[i], in_send.at[i], in_recv.at[i]))
-
-    send_in(1)
+    send_in(0, SPACE)
+    send_in(1, PLANE + SPACE)
+    for i in range(2, CHUNKS):
+        send_in(i, SHIFTS)
+    def cross(n):
+        return pltpu.make_async_remote_copy(
+            src_ref=given.at[n],
+            dst_ref=taken.at[n],
+            send_sem=x_send.at[n],
+            recv_sem=x_recv.at[n],
+            device_id=partner,
+            device_id_type=MESH,
+        )
+
+    def send_out(i):
+        def repack(b, carry):
+            rows = pl.ds(pl.multiple_of(b * 8, 8), 8)
+            block = jnp.concatenate([back_f[t, rows, :] for t in range(4)], axis=1)
+            for k in range(8 // NW):
+                back[i, b * (8 // NW) + k] = fold(block[k * NW : (k + 1) * NW]).astype(BF16)
+            return carry
+
+        lax.fori_loop(0, ROWS // 8, repack, 0, unroll=2)
+        send(places, SHIFTS, back.at[i], home.at[i], out_send.at[i], out_recv.at[i])
+        pltpu.make_async_copy(back.at[i, me], home.at[i, me], own_sem.at[i]).start()
+
     loads[2].wait()
     loads[3].wait()
 
     for i in range(CHUNKS):
         wait_all(got.at[i], in_recv.at[i])
-        if i + 2 < CHUNKS:
-            send_in(i + 2)
         base = (i % KEEP) * ROWS
         kept = slice(base, base + ROWS)
 
@@ -280,40 +290,18 @@
         lax.fori_loop(0, NW // TOGETHER, attention, 0)
 
         if i % KEEP == KEEP - 1:
-            for n in range(3):
+            for n in range(4):
                 columns = slice(n * D, (n + 1) * D)
-                term = dot_0(normed[...], dqkv[:, columns])
+                if n < 3:
+                    term = dot_0(normed[...], dqkv[:, columns])
+                else:
+                    term = dot_0(att[...], cot_w[...])
                 dw[:, columns] = term if i < KEEP else dw[:, columns] + term
-            term = dot_0(att[...], cot_w[...])
-            dwo[...] = term if i < KEEP else dwo[...] + term
-
-        if i == CHUNKS - 1:
-
-            def regroup(owner_core):
-                def step(t, carry):
-                    x, y_lo, y_hi, half = t // 8, (t // 4) % 2, (t // 2) % 2, t % 2
-                    tile = x * 16 + y_lo * 8 + owner_core * 4 + y_hi * 2 + half
-                    rows = pl.ds(pl.multiple_of(tile * 8, 8), 8)
-                    blocks = [dw[rows, n * D : (n + 1) * D] for n in range(3)] + [dwo[rows, :]]
-                    chip = chip_of(x, y_hi * 2 + y_lo, half * 2)
-                    for k in range(2):
-                        piece = [b[k * 4 : (k + 1) * 4] for b in blocks]
-                        part[owner_core, chip + k] = jnp.concatenate(piece, axis=0).astype(BF16)
-                    return carry
-
-                lax.fori_loop(0, CHIPS // 2, step, 0, unroll=2)
-
-            regroup(1 - core)
-            cross = pltpu.make_async_remote_copy(
-                src_ref=part.at[1 - core],
-                dst_ref=other,
-                send_sem=x_send,
-                recv_sem=x_recv,
-                device_id=partner,
-                device_id_type=MESH,
-            )
-            cross.start()
-            regroup(core)
+                if i == CHUNKS - 1:
+                    for b in range(8):
+                        rows = pl.ds(pl.multiple_of(b * 64 + (1 - core) * 32, 32), 32)
+                        given[n, b] = dw[rows, columns].astype(BF16)
+                    cross(n).start()
 
         gnorm[...] = dot_t(dqkv[kept, :], wqkv[...])
         for j in range(NW):
@@ -328,46 +316,118 @@
             for t in range(4):
                 back_f[t, members, :] = result[:, t * 128 : (t + 1) * 128]
 
-        def repack(b, carry):
-            rows = pl.ds(pl.multiple_of(b * 8, 8), 8)
-            block = jnp.concatenate([back_f[t, rows, :] for t in range(4)], axis=1)
-            for k in range(8 // NW):
-                back[i, b * (8 // NW) + k] = fold(block[k * NW : (k + 1) * NW]).astype(BF16)
+        if i < CHUNKS - 1:
+            send_out(i)
+
+    send_out(CHUNKS - 1)
+    for n in range(4):
+        cross(n).wait_recv()
+
+    def halves(owner_x):
+        def step(b, carry):
+            y_lo, y_hi = b // 2, b % 2
+            block = owner_x * 2 + y_lo
+            rows = pl.ds(pl.multiple_of(block * 64 + core * 32 + y_hi * 16, 16), 16)
+            half = pl.ds(pl.multiple_of(y_hi * 16, 16), 16)
+            mine = [
+                dw[rows, n * D : (n + 1) * D] + taken[n, block, half, :].astype(F32) for n in range(4)
+            ]
+            y = y_hi * 2 + y_lo
+            for z in range(4):
+                piece = jnp.concatenate([m[z * 4 : (z + 1) * 4] for m in mine], axis=0).astype(BF16)
+                chip = owner_x * 16 + y * 4 + z
+                slots = (chip, y * 16 + owner_x * 4 + z, z * 16 + owner_x * 4 + y, chip)
+                for a in range(4):
+                    parts[a, slots[a]] = piece[:, a * 128 : (a + 1) * 128]
             return carry
 
-        lax.fori_loop(0, ROWS // 8, repack, 0, unroll=2)
-        for_all(here, sender(here, back.at[i], home.at[i], out_send.at[i], out_recv.at[i]))
-        pltpu.make_async_copy(back.at[i, me], home.at[i, me], own_sem.at[i]).start()
-
-    cross.wait_recv()
-
-    def pair(b, carry):
-        for k in range(4):
-            p = b * 4 + k
-            summed[p] = (part[core, p].astype(F32) + other[p].astype(F32)).astype(BF16)
-        return carry
-
-    lax.fori_loop(0, CHIPS // 4, pair, 0)
-    for_all(here, sender(here, summed, pieces, r_send, r_recv))
-    pieces[me] = summed[me]
+        lax.fori_loop(0, 4, step, 0)
+
+    def along(a, d):
+        there = moved(here, *(d if n == a else 0 for n in range(3)))
+        pltpu.make_async_remote_copy(
+            src_ref=parts.at[a, pl.ds(pl.multiple_of(there[a] * 16, 16), 16)],
+            dst_ref=line_in.at[a, here[a]],
+            send_sem=a_send.at[a],
+            recv_sem=a_recv.at[a],
+            device_id=device(*there),
+            device_id_type=MESH,
+        ).start()
+
+    for d in range(1, 4):
+        halves((here[0] + d) % 4)
+        along(0, d)
+    halves(here[0])
+    for d in range(1, 4):
+        along(1, d)
+        along(2, d)
+    send(places, SHIFTS, parts.at[3], straight, r_send, r_recv)
+    straight[me] = parts[3, me]
+
+    def three(buffer, sem):
+        part = buffer.at[pl.ds(0, 3)]
+        pltpu.make_async_copy(part, part, sem).wait()
+
+    def fifteen(buffer, sem):
+        part = buffer.at[pl.ds(0, 15)]
+        pltpu.make_async_copy(part, part, sem).wait()
+
+    across = ((1, 2), (0, 2), (0, 1))
+    for a in range(3):
+        three(line_in.at[a], a_recv.at[a])
+        p, q = across[a]
+
+        def plane_sum(k, carry):
+            value = parts[a, here[a] * 16 + k].astype(F32)
+            for d in range(1, 4):
+                value = value + line_in[a, (here[a] + d) % 4, k].astype(F32)
+            line_sum[a, k] = value.astype(BF16)
+            return carry
+
+        lax.fori_loop(0, 16, plane_sum, 0, unroll=4)
+        own = here[p] * 4 + here[q]
+        landing = plane_in.at[a, own]
+        for s in PLANE_SHIFTS:
+            shift = [0, 0, 0]
+            shift[p], shift[q] = s
+            there = places.at(shift)
+            pltpu.make_async_remote_copy(
+                src_ref=line_sum.at[a, there[p] * 4 + there[q]],
+                dst_ref=landing,
+                send_sem=b_send.at[a],
+                recv_sem=b_recv.at[a],
+                device_id=places.device(shift),
+                device_id_type=MESH,
+            ).start()
+        plane_in[a, own] = line_sum[a, own]
 
     for i in range(CHUNKS):
         wait_all(home.at[i], out_recv.at[i])
         pltpu.make_async_copy(back.at[i, me], home.at[i, me], own_sem.at[i]).wait()
-    wait_all(pieces, r_recv)
-
-    def add(b, acc):
-        for k in range(4):
-            acc = acc + pieces[b * 4 + k].astype(F32)
+    wait_all(straight, r_recv)
+
+    def add(k, acc):
+        for n in range(8):
+            acc = acc + straight[k * 8 + n].astype(F32)
         return acc
 
-    total_ref[...] = lax.fori_loop(0, CHIPS // 4, add, jnp.zeros((16, D), F32))
-
-    cross.wait_send()
+    total_ref[:, 3 * 128 :] = lax.fori_loop(0, CHIPS // 8, add, jnp.zeros((16, 128), F32))
+    for a in range(3):
+        fifteen(plane_in.at[a], b_recv.at[a])
+        value = plane_in[a, 0].astype(F32)
+        for k in range(1, 16):
+            value = value + plane_in[a, k].astype(F32)
+        total_ref[:, a * 128 : (a + 1) * 128] = value
+
+    for n in range(4):
+        cross(n).wait_send()
     for i in range(CHUNKS):
         wait_all(sent.at[i], in_send.at[i])
         wait_all(back.at[i], out_send.at[i])
-    wait_all(summed, r_send)
+    for a in range(3):
+        three(line_in.at[a], a_send.at[a])
+        fifteen(plane_in.at[a], b_send.at[a])
+    wait_all(straight, r_send)
 
 
 def finish(home, total, gt, gw, gwo):
@@ -378,7 +438,7 @@
         gt[b // 4, pl.ds(pl.multiple_of((b % 4) * 16, 16), 16)] = value.astype(BF16)
         return carry
 
-    lax.fori_loop(0, 16, cells, 0, unroll=4)
+    lax.fori_loop(0, home.shape[1], cells, 0, unroll=4)
 
     @pl.when(pl.program_id(0) == 0)
     def _():
@@ -420,16 +480,20 @@
             vmem((ROWS, D), F32),
             vmem((4, ROWS, 128), F32),
             vmem((CHUNKS, CHIPS, 16, OUT_LANES), BF16),
-            vmem((D, 3 * D), F32),
-            vmem((D, D), F32),
-            vmem((2, CHIPS, 16, D), BF16),
-            vmem((CHIPS, 16, D), BF16),
-            vmem((CHIPS, 16, D), BF16),
-            vmem((CHIPS, 16, D), BF16),
+            vmem((D, 4 * D), F32),
+            vmem((4, 8, 32, D), BF16),
+            vmem((4, 8, 32, D), BF16),
+            vmem((4, CHIPS, 16, 128), BF16),
+            vmem((3, 4, 16, 16, 128), BF16),
+            vmem((3, 16, 16, 128), BF16),
+            vmem((3, 16, 16, 128), BF16),
+            vmem((CHIPS, 16, 128), BF16),
             dma((4,)), regular, regular, dma((CHUNKS,)),
             dma((CHUNKS,)), dma((CHUNKS,)),
             dma((CHUNKS,)), dma((CHUNKS,)),
-            dma(()), dma(()),
+            dma((4,)), dma((4,)),
+            dma((3,)), dma((3,)),
+            dma((3,)), dma((3,)),
             dma(()), dma(()),
         ],
         compiler_params=pltpu.CompilerParams(
@@ -437,7 +501,7 @@
         ),
         name="grid_attention_backward",
     )(tokens, cotangent, w_qkv, w_out)
-    steps = 4
+    steps = 2
     return pl.pallas_call(
         finish,
         grid=(steps,),

time: 72.3 us -> 60.6 us (0.84)
  Pallas kernels: 71 us -> 59.9 us
    pallas_call x1, Pallas kernels: 67.5 us -> 57.5 us  [body(): pl.pallas_call(kernel, out_shape=(jax.ShapeDtypeStruct((CHUNKS, CHIPS, 16...]
    pallas_call x1, Pallas kernels: 3.56 us -> 2.41 us  [body(): pl.pallas_call(finish, grid=(steps,), out_shape=(jax.ShapeDtypeStruct((ro...]
where the time goes in v3:
time: 60.6 us; the launch traced here: 60.5 us
  Pallas kernels  59.9 us (99%)
  between operations  0.64 us (1%)
    pallas_call x1, Pallas kernels, body(): pl.pallas_call(kernel, out_shape=(jax.ShapeDtypeStruct((CHUNKS, CHIPS, 16...  57.5 us
    pallas_call x1, Pallas kernels, body(): pl.pallas_call(finish, grid=(steps,), out_shape=(jax.ShapeDtypeStruct((ro...  2.41 us

profile of v3, /device:TPU:0, one launch (start us, length us, event | category | flops | bytes accessed | tf_op | source)
XLA Modules:
  0.0 60.5 jit_solution(6900467363394118746)
XLA Ops:
  0.6 57.5 %grid_attention_backward.1 = (bf16[4,64,16,128]{3,2,1,0:T(8,128)(2,1)}, f32[16,512]{1,0:T(8,128)}) custom-call(bf16[16,64,512]{2,1,0:T(8,128)(2,1)} %tok_hbm.1, bf16[16,64,512]{2,1,0:T(8,128)(2,1)} %cot_hbm.1, bf16[512,1536]{1,0:T(8,128)(2,1)} %wqkv_hbm.1, bf16[512,512]{1,0:T(8,128)(2,1)} %wout_hbm.1), custom_call_target="tpu_custom_call" | custom-call | tf_op jit(solution)/shard_map/grid_attention_backward/pallas_call | solution.py:456
  58.1 2.4 %cells_from_blocks.1 = (bf16[16,64,512]{2,1,0:T(8,128)(2,1)}, f32[4,1536]{1,0:T(4,128)}, f32[4,512]{1,0:T(4,128)}) custom-call(bf16[4,64,16,128]{3,2,1,0:T(8,128)(2,1)} %get-tuple-element.5.home, f32[16,512]{1,0:T(8,128)} %get-tuple-element.6.total), custom_call_target="tpu_custom_call" | custom-call | tf_op jit(solution)/shard_map/cells_from_blocks/pallas_call | solution.py:505

commit v4 on v3

--- a/solution.py
+++ b/solution.py
@@ -211,16 +211,15 @@
 
     pl.semaphore_wait(barrier, 10)
     signal(line_sem, LINE)
-    for i in range(2):
+    for i in range(CHUNKS):
         send_in(i, LINE)
     pl.semaphore_wait(line_sem, 9)
     signal(space_sem, [(d, 0, 0) for d in range(1, 4)])
     send_in(0, PLANE)
     pl.semaphore_wait(space_sem, 3)
     send_in(0, SPACE)
-    send_in(1, PLANE + SPACE)
-    for i in range(2, CHUNKS):
-        send_in(i, SHIFTS)
+    for i in range(1, CHUNKS):
+        send_in(i, PLANE + SPACE)
     def cross(n):
         return pltpu.make_async_remote_copy(
             src_ref=given.at[n],
@@ -289,13 +288,14 @@
 
         lax.fori_loop(0, NW // TOGETHER, attention, 0)
 
-        if i % KEEP == KEEP - 1:
+        if i > 0:
+            used = slice(0, (i + 1) * ROWS) if i < KEEP else kept
             for n in range(4):
                 columns = slice(n * D, (n + 1) * D)
                 if n < 3:
-                    term = dot_0(normed[...], dqkv[:, columns])
+                    term = dot_0(normed[used, :], dqkv[used, columns])
                 else:
-                    term = dot_0(att[...], cot_w[...])
+                    term = dot_0(att[used, :], cot_w[used, :])
                 dw[:, columns] = term if i < KEEP else dw[:, columns] + term
                 if i == CHUNKS - 1:
                     for b in range(8):
@@ -341,7 +341,7 @@
                     parts[a, slots[a]] = piece[:, a * 128 : (a + 1) * 128]
             return carry
 
-        lax.fori_loop(0, 4, step, 0)
+        lax.fori_loop(0, 4, step, 0, unroll=2)
 
     def along(a, d):
         there = moved(here, *(d if n == a else 0 for n in range(3)))

time: 60.6 us -> 59.8 us (0.987)
  Pallas kernels: 59.9 us -> 59 us
    pallas_call x1, Pallas kernels: 57.5 us -> 56.6 us  [body(): pl.pallas_call(kernel, out_shape=(jax.ShapeDtypeStruct((CHUNKS, CHIPS, 16...]
where the time goes in v4:
time: 59.8 us; the launch traced here: 59.6 us
  Pallas kernels  59 us (99%)
  between operations  0.64 us (1%)
    pallas_call x1, Pallas kernels, body(): pl.pallas_call(kernel, out_shape=(jax.ShapeDtypeStruct((CHUNKS, CHIPS, 16...  56.6 us
    pallas_call x1, Pallas kernels, body(): pl.pallas_call(finish, grid=(steps,), out_shape=(jax.ShapeDtypeStruct((ro...  2.41 us

profile of v4, /device:TPU:0, one launch (start us, length us, event | category | flops | bytes accessed | tf_op | source)
XLA Modules:
  0.0 59.6 jit_solution(12592329880553683134)
XLA Ops:
  0.6 56.6 %grid_attention_backward.1 = (bf16[4,64,16,128]{3,2,1,0:T(8,128)(2,1)}, f32[16,512]{1,0:T(8,128)}) custom-call(bf16[16,64,512]{2,1,0:T(8,128)(2,1)} %tok_hbm.1, bf16[16,64,512]{2,1,0:T(8,128)(2,1)} %cot_hbm.1, bf16[512,1536]{1,0:T(8,128)(2,1)} %wqkv_hbm.1, bf16[512,512]{1,0:T(8,128)(2,1)} %wout_hbm.1), custom_call_target="tpu_custom_call" | custom-call | tf_op jit(solution)/shard_map/grid_attention_backward/pallas_call | solution.py:456
  57.2 2.4 %cells_from_blocks.1 = (bf16[16,64,512]{2,1,0:T(8,128)(2,1)}, f32[4,1536]{1,0:T(4,128)}, f32[4,512]{1,0:T(4,128)}) custom-call(bf16[4,64,16,128]{3,2,1,0:T(8,128)(2,1)} %get-tuple-element.5.home, f32[16,512]{1,0:T(8,128)} %get-tuple-element.6.total), custom_call_target="tpu_custom_call" | custom-call | tf_op jit(solution)/shard_map/cells_from_blocks/pallas_call | solution.py:505
